TPU v7x, 256 devices: a whole 4x4x8 slice. The times are simulated.
256 devices in a mesh: frame: 16 (over z, x_hi), row: 16 (over x_lo, y, core).
Axes of the slice: x: 4 (x_hi: 2, x_lo: 2; x = x_hi * 2 + x_lo), y: 4, z: 8, core: 2. Of those that a mesh axis runs over, the one named last changes fastest.
Arguments:
- latents: float32 [32, 64, 112, 320], P('frame', 'row'), may hold values from -8 to 8, as said below
- hint: float32 [32, 64, 112, 320], P('frame', 'row'), may hold values from -6 to 6
- norm_gains: float32 [4, 320], replicated, may hold values from 0.1 to 1.9
- norm_shifts: float32 [4, 320], replicated, may hold values from -3 to 3
- spatial_kernels: float32 [2, 3, 3, 320, 320], replicated, may hold values from -0.109375 to 0.109375
- temporal_kernels: float32 [2, 3, 320, 320], replicated, may hold values from -0.1875 to 0.1875
- zero_weight: float32 [320, 320], replicated, may hold values from -0.3125 to 0.3125
Outputs:
- block_out: float32 [32, 64, 112, 320], P('frame', 'row')
Inputs may be any that keep to these rules, and one draw needn't show every extreme that they name: latents are real-valued activations of order one.
All inputs are finite; a program needn't handle non-finite values.
Results may differ from a plain program's by a relative error of at most 0.0001.
Values sent between devices are 32-bit elements; how exact they have to be, the bound alone decides.
A program may use at most 128 MiB of HBM per device.

v0:
```python
import jax
import jax.numpy as jnp
from jax import lax
from jax.sharding import PartitionSpec as P

GROUPS = 32


EPS = 1e-05
HIGH = lax.Precision.HIGHEST


def extended(shard, sides, width):
    for axis, dim in sides:
        count, length = (lax.axis_size(axis), shard.shape[dim])
        up = [(i, (i + 1) % count) for i in range(count - 1)]
        down = [(j, i) for i, j in up]
        last = lax.slice_in_dim(shard, length - width, length, axis=dim)
        first = lax.slice_in_dim(shard, 0, width, axis=dim)
        before = lax.ppermute(last, axis, up)
        after = lax.ppermute(first, axis, down)
        shard = jnp.concatenate([before, shard, after], axis=dim)
    return shard


def group_moments(value):
    width = value.shape[-1]
    grouped = value.reshape(-1, GROUPS, width // GROUPS)
    count = grouped.shape[0] * grouped.shape[2] * lax.axis_size("frame") * lax.axis_size("row")
    totals = lax.psum(jnp.sum(grouped, axis=(0, 2)), ("frame", "row"))
    mean = totals / count
    centred = grouped - mean[None, :, None]
    variance = lax.psum(jnp.sum(centred * centred, axis=(0, 2)), ("frame", "row")) / count
    return (mean, variance)


def activate(value, mean, variance, gain, shift):
    shape = value.shape
    grouped = value.reshape(shape[:-1] + (GROUPS, shape[-1] // GROUPS))
    normed = (grouped - mean[:, None]) * lax.rsqrt(variance + EPS)[:, None]
    return jax.nn.silu(normed.reshape(shape) * gain + shift)


def spatial_taps(padded_rows, kernel):
    rows = padded_rows.shape[1] - 2
    cols = padded_rows.shape[2]
    padded = jnp.pad(padded_rows, ((0, 0), (0, 0), (1, 1), (0, 0)))
    total = jnp.zeros((padded_rows.shape[0], rows, cols, kernel.shape[-1]), jnp.float32)
    for shift_y in range(3):
        for shift_x in range(3):
            total = total + jnp.einsum(
                "fhwc,cd->fhwd",
                padded[:, shift_y : shift_y + rows, shift_x : shift_x + cols],
                kernel[shift_y, shift_x],
                precision=HIGH,
            )
    return total


def temporal(value, kernel):
    frames = value.shape[0]
    padded = extended(value, (("frame", 0),), 1)
    total = jnp.zeros(value.shape, jnp.float32)
    for tap in range(3):
        total = total + jnp.einsum(
            "fhwc,cd->fhwd", padded[tap : tap + frames], kernel[tap], precision=HIGH
        )
    return total


def local(latents, hint, norm_gains, norm_shifts, spatial_kernels, temporal_kernels, zero_weight):
    control_in = latents + hint
    mean, variance = group_moments(control_in)
    active = activate(control_in, mean, variance, norm_gains[0], norm_shifts[0])
    inner = spatial_taps(extended(active, (("row", 1),), 1), spatial_kernels[0])
    mean, variance = group_moments(inner)
    active = activate(inner, mean, variance, norm_gains[1], norm_shifts[1])
    control_out = control_in + temporal(active, temporal_kernels[0])
    skip = latents + jnp.einsum("fhwc,cd->fhwd", control_out, zero_weight, precision=HIGH)
    mean, variance = group_moments(skip)
    middle = activate(skip, mean, variance, norm_gains[2], norm_shifts[2])
    padded = extended(middle, (("row", 1),), 1)
    inner = spatial_taps(padded, spatial_kernels[1])
    mean, variance = group_moments(inner)
    active = activate(inner, mean, variance, norm_gains[3], norm_shifts[3])
    return skip + temporal(active, temporal_kernels[1])


def solution(mesh):
    return jax.shard_map(
        local,
        mesh=mesh,
        in_specs=(
            P("frame", "row", None, None),
            P("frame", "row", None, None),
            P(),
            P(),
            P(),
            P(),
            P(),
        ),
        out_specs=P("frame", "row", None, None),
        check_vma=False,
    )
```

profile of v0, /device:TPU:1, one launch (start us, length us, event | category | flops | bytes accessed | tf_op | source)
XLA Modules:
  0.0 770.7 jit_solution(2465426118178999496)
XLA Ops:
  0.0 2.0 fusion.108
  2.2 81.4 %psum.56 = f32[32]{0:T(128)S(1)} all-reduce(f32[32]{0:T(128)S(1)} %reduce_sum.97), channel_id=1, replica_groups=mesh['frame'=16,'row'=16] {'frame','row'}, use_global_device_ids=true, to_apply=%region_2.0 | all-reduce | flops 32 | bytes 256 | tf_op jit(solution)/shard_map/psum | solution.py:30
  83.9 0.3 multiply_reduce_fusion.3
  84.4 72.4 %psum.57 = f32[32]{0:T(128)S(1)} all-reduce(f32[32]{0:T(128)S(1)} %reduce_sum.100), channel_id=1, replica_groups=mesh['frame'=16,'row'=16] {'frame','row'}, use_global_device_ids=true, to_apply=%region_5.6 | all-reduce | flops 32 | bytes 256 | tf_op jit(solution)/shard_map/psum | solution.py:33
  157.1 0.6 divide_multiply_fusion.3
  157.7 0.9 fusion.113
  158.6 2.8 collective-permute-start
  161.3 2.3 collective-permute-start.1
  163.6 7.8 %fusion.109 = (f32[1,3,3,320,320]{4,3,2,1,0:T(8,128)}, f32[1,3,3,320,320]{4,3,2,1,0:T(8,128)}) fusion(f32[2,3,3,320,320]{4,3,2,1,0:T(8,128)} %param.11), kind=kLoop, calls=%fused_computation.150 | loop fusion | bytes 14745600 | tf_op jit(solution)/shard_map/slice | solution.py:83
  171.4 6.2 copy.46
  177.6 3.5 fusion.84
  181.1 1.6 select_maximum_fusion.2
  182.7 2.3 fusion.78
  185.0 2.5 fusion.80
  187.4 2.5 fusion.73
  189.9 2.3 fusion.75
  192.2 3.7 fusion.17
  195.9 2.5 fusion.47
  198.5 2.3 fusion.21
  200.8 2.9 fusion.114
  203.9 76.1 %psum.58 = f32[32]{0:T(128)S(1)} all-reduce(f32[32]{0:T(128)S(1)} %reduce_sum.106), channel_id=1, replica_groups=mesh['frame'=16,'row'=16] {'frame','row'}, use_global_device_ids=true, to_apply=%region_8.9 | all-reduce | flops 32 | bytes 256 | tf_op jit(solution)/shard_map/psum | solution.py:30
  280.2 0.3 multiply_reduce_fusion.2
  280.6 0.1 reduce_sum.112
  280.8 72.7 %psum.59 = f32[32]{0:T(128)S(1)} all-reduce(f32[32]{0:T(128)S(1)} %reduce_sum.112), channel_id=1, replica_groups=mesh['frame'=16,'row'=16] {'frame','row'}, use_global_device_ids=true, to_apply=%region_11.12 | all-reduce | flops 32 | bytes 256 | tf_op jit(solution)/shard_map/psum | solution.py:33
  353.7 0.6 divide_multiply_fusion.2
  354.4 1.4 collective-permute-start.3
  355.8 5.5 collective-permute-start.2
  361.4 2.3 fusion.90
  363.7 9.8 %collective-permute-done.3 = f32[1,4,112,320]{2,3,1,0:T(8,128)S(1)} collective-permute-done((f32[1,4,112,320]{2,3,1,0:T(8,128)S(1)}, f32[1,4,112,320]{2,3,1,0:T(8,128)S(1)}, u32[]{:S(2)}, u32[]{:S(2)}) %collective-permute-start.3) | collective-permute-done | bytes 573472 | tf_op jit(solution)/shard_map/ppermute | solution.py:21
  373.5 2.4 fusion.4
  375.9 11.1 %collective-permute-done.2 = f32[1,4,112,320]{2,3,1,0:T(8,128)S(1)} collective-permute-done((f32[1,4,112,320]{2,3,1,0:T(8,128)S(1)}, f32[1,4,112,320]{2,3,1,0:T(8,128)S(1)}, u32[]{:S(2)}, u32[]{:S(2)}) %collective-permute-start.2) | collective-permute-done | bytes 573472 | tf_op jit(solution)/shard_map/ppermute | solution.py:20
  387.0 2.6 fusion.57
  389.6 2.5 fusion.115
  392.2 0.1 reduce_sum.115
  392.3 77.7 %psum.60 = f32[32]{0:T(128)S(1)} all-reduce(f32[32]{0:T(128)S(1)} %reduce_sum.115), channel_id=1, replica_groups=mesh['frame'=16,'row'=16] {'frame','row'}, use_global_device_ids=true, to_apply=%region_14.15 | all-reduce | flops 32 | bytes 256 | tf_op jit(solution)/shard_map/psum | solution.py:30
  470.2 0.3 multiply_reduce_fusion.1
  470.8 6.1 copy.47
  476.8 72.7 %psum.61 = f32[32]{0:T(128)S(1)} all-reduce(f32[32]{0:T(128)S(1)} %reduce_sum.145), channel_id=1, replica_groups=mesh['frame'=16,'row'=16] {'frame','row'}, use_global_device_ids=true, to_apply=%region_17.18 | all-reduce | flops 32 | bytes 256 | tf_op jit(solution)/shard_map/psum | solution.py:33
  549.7 0.6 divide_multiply_fusion.1
  550.4 3.0 collective-permute-start.4
  553.3 2.3 collective-permute-start.5
  555.7 3.5 fusion.83
  559.2 2.6 collective-permute-done.5
  561.7 0.6 select_maximum_fusion
  562.3 2.4 fusion.70
  564.8 2.3 fusion.68
  567.1 2.3 fusion.65
  569.4 2.5 fusion.63
  571.9 2.5 fusion.25
  574.4 2.5 fusion.53
  576.9 2.3 fusion.29
  579.3 2.9 fusion.116
  582.4 76.4 %psum.62 = f32[32]{0:T(128)S(1)} all-reduce(f32[32]{0:T(128)S(1)} %reduce_sum.148), channel_id=1, replica_groups=mesh['frame'=16,'row'=16] {'frame','row'}, use_global_device_ids=true, to_apply=%region_20.21 | all-reduce | flops 32 | bytes 256 | tf_op jit(solution)/shard_map/psum | solution.py:30
  659.0 0.3 multiply_reduce_fusion
  659.4 0.1 reduce_sum.151
  659.5 73.8 %psum.63 = f32[32]{0:T(128)S(1)} all-reduce(f32[32]{0:T(128)S(1)} %reduce_sum.151), channel_id=1, replica_groups=mesh['frame'=16,'row'=16] {'frame','row'}, use_global_device_ids=true, to_apply=%region_23.24 | all-reduce | flops 32 | bytes 256 | tf_op jit(solution)/shard_map/psum | solution.py:33
  733.6 0.6 divide_multiply_fusion
  734.3 1.4 collective-permute-start.7
  735.7 5.5 collective-permute-start.6
  741.2 2.3 fusion.86
  743.6 9.8 %collective-permute-done.7 = f32[1,4,112,320]{2,3,1,0:T(8,128)S(1)} collective-permute-done((f32[1,4,112,320]{2,3,1,0:T(8,128)S(1)}, f32[1,4,112,320]{2,3,1,0:T(8,128)S(1)}, u32[]{:S(2)}, u32[]{:S(2)}) %collective-permute-start.7) | collective-permute-done | bytes 573472 | tf_op jit(solution)/shard_map/ppermute | solution.py:21
  753.4 2.4 fusion.12
  755.8 11.1 %collective-permute-done.6 = f32[1,4,112,320]{2,3,1,0:T(8,128)S(1)} collective-permute-done((f32[1,4,112,320]{2,3,1,0:T(8,128)S(1)}, f32[1,4,112,320]{2,3,1,0:T(8,128)S(1)}, u32[]{:S(2)}, u32[]{:S(2)}) %collective-permute-start.6) | collective-permute-done | bytes 573472 | tf_op jit(solution)/shard_map/ppermute | solution.py:20
  766.9 3.6 fusion.60
  (62 shorter events, 3.2 us)
Async XLA Ops:
  0.0 389.6 %copy-start = (f32[320,320]{1,0:T(8,128)S(1)}, f32[320,320]{1,0:T(8,128)}, u32[]{:S(2)}) copy-start(f32[320,320]{1,0:T(8,128)} %param.13) | copy-start | bytes 1228804
  2.0 155.0 %copy-start.7 = (f32[4,320]{1,0:T(4,128)S(1)}, f32[4,320]{1,0:T(4,128)}, u32[]{:S(2)}) copy-start(f32[4,320]{1,0:T(4,128)} %param.10) | copy-start | bytes 15364
  2.0 155.0 %copy-start.8 = (f32[4,320]{1,0:T(4,128)S(1)}, f32[4,320]{1,0:T(4,128)}, u32[]{:S(2)}) copy-start(f32[4,320]{1,0:T(4,128)} %param.9) | copy-start | bytes 15364
  158.6 22.5 %collective-permute-start = (f32[2,1,112,320]{2,3,1,0:T(8,128)}, f32[2,1,112,320]{2,3,1,0:T(8,128)}, u32[]{:S(2)}, u32[]{:S(2)}) collective-permute-start(f32[2,1,112,320]{2,3,1,0:T(8,128)} %get-tuple-element.23), channel_id=1, source_target_pairs={{0,1},{1,2},{2,3},{3,4},{4,5},{5,6},{6,7},{7,8},{8,9},{9,10},{10,1... | collective-permute-start | bytes 860168 | tf_op jit(solution)/shard_map/ppermute | solution.py:20
  161.3 19.8 %collective-permute-start.1 = (f32[2,1,112,320]{2,3,1,0:T(8,128)}, f32[2,1,112,320]{2,3,1,0:T(8,128)S(1)}, u32[]{:S(2)}, u32[]{:S(2)}) collective-permute-start(f32[2,1,112,320]{2,3,1,0:T(8,128)} %get-tuple-element.24), channel_id=1, source_target_pairs={{1,0},{2,1},{3,2},{4,3},{5,4},{6,5},{7,6},{8,7},{9,8},{10,9},{11,1... | collective-permute-start | bytes 860168 | tf_op jit(solution)/shard_map/ppermute | solution.py:21
  177.6 5.1 copy-start.3
  353.7 7.7 copy-start.5
  354.4 19.1 %collective-permute-start.3 = (f32[1,4,112,320]{2,3,1,0:T(8,128)S(1)}, f32[1,4,112,320]{2,3,1,0:T(8,128)S(1)}, u32[]{:S(2)}, u32[]{:S(2)}) collective-permute-start(f32[1,4,112,320]{2,3,1,0:T(8,128)S(1)} %get-tuple-element.22), channel_id=1, source_target_pairs={{16,0},{32,16},{48,32},{64,48},{80,64},{96,80},{112,96},{128,112},... | collective-permute-start | bytes 1720328 | tf_op jit(solution)/shard_map/ppermute | solution.py:21
  355.8 31.2 %collective-permute-start.2 = (f32[1,4,112,320]{2,3,1,0:T(8,128)S(1)}, f32[1,4,112,320]{2,3,1,0:T(8,128)S(1)}, u32[]{:S(2)}, u32[]{:S(2)}) collective-permute-start(f32[1,4,112,320]{2,3,1,0:T(8,128)S(1)} %get-tuple-element.21), channel_id=1, source_target_pairs={{0,16},{16,32},{32,48},{48,64},{64,80},{80,96},{96,112},{112,128},... | collective-permute-start | bytes 1720328 | tf_op jit(solution)/shard_map/ppermute | solution.py:20
  375.9 13.7 %copy-start.4 = (f32[2,4,112,320]{2,3,1,0:T(8,128)S(1)}, f32[2,4,112,320]{2,3,1,0:T(8,128)}, u32[]{:S(2)}) copy-start(f32[2,4,112,320]{2,3,1,0:T(8,128)} %param.7) | copy-start | bytes 3440644
  550.4 8.8 %collective-permute-start.4 = (f32[2,1,112,320]{2,3,1,0:T(8,128)S(1)}, f32[2,1,112,320]{2,3,1,0:T(8,128)S(1)}, u32[]{:S(2)}, u32[]{:S(2)}) collective-permute-start(f32[2,1,112,320]{2,3,1,0:T(8,128)S(1)} %get-tuple-element.19), channel_id=1, source_target_pairs={{0,1},{1,2},{2,3},{3,4},{4,5},{5,6},{6,7},{7,8},{8,9},{9,10},{10,1... | collective-permute-start | bytes 860168 | tf_op jit(solution)/shard_map/ppermute | solution.py:20
  553.3 8.4 %collective-permute-start.5 = (f32[2,1,112,320]{2,3,1,0:T(8,128)S(1)}, f32[2,1,112,320]{2,3,1,0:T(8,128)S(1)}, u32[]{:S(2)}, u32[]{:S(2)}) collective-permute-start(f32[2,1,112,320]{2,3,1,0:T(8,128)S(1)} %get-tuple-element.20), channel_id=1, source_target_pairs={{1,0},{2,1},{3,2},{4,3},{5,4},{6,5},{7,6},{8,7},{9,8},{10,9},{11,1... | collective-permute-start | bytes 860168 | tf_op jit(solution)/shard_map/ppermute | solution.py:21
  555.7 6.6 copy-start.2
  733.5 7.7 copy-start.6
  734.3 19.1 %collective-permute-start.7 = (f32[1,4,112,320]{2,3,1,0:T(8,128)S(1)}, f32[1,4,112,320]{2,3,1,0:T(8,128)S(1)}, u32[]{:S(2)}, u32[]{:S(2)}) collective-permute-start(f32[1,4,112,320]{2,3,1,0:T(8,128)S(1)} %get-tuple-element.18), channel_id=1, source_target_pairs={{16,0},{32,16},{48,32},{64,48},{80,64},{96,80},{112,96},{128,112},... | collective-permute-start | bytes 1720328 | tf_op jit(solution)/shard_map/ppermute | solution.py:21
  735.7 31.2 %collective-permute-start.6 = (f32[1,4,112,320]{2,3,1,0:T(8,128)S(1)}, f32[1,4,112,320]{2,3,1,0:T(8,128)S(1)}, u32[]{:S(2)}, u32[]{:S(2)}) collective-permute-start(f32[1,4,112,320]{2,3,1,0:T(8,128)S(1)} %get-tuple-element.17), channel_id=1, source_target_pairs={{0,16},{16,32},{32,48},{48,64},{64,80},{80,96},{96,112},{112,128},... | collective-permute-start | bytes 1720328 | tf_op jit(solution)/shard_map/ppermute | solution.py:20
  766.9 3.6 copy-start.1
where the time goes:
time: 779 us; the launch traced here: 771 us
  blocking collectives  603 us (77%)
  matrix products  65.7 us (8%)
  waiting for transfers between devices  44.4 us (6%)
  starting transfers between devices  24.3 us (3%)
  local copies, waits for them, and re-layouts  23.5 us (3%)
  other arithmetic  8.81 us (1%)
    psum x4, blocking collectives, group_moments(): totals = lax.psum(jnp.sum(grouped, axis=(0, 2)), ('frame', 'row'))  312 us
    psum x4, blocking collectives, group_moments(): lax.psum(jnp.sum(centred * centred, axis=(0, 2)), ('frame', 'row')) / count  292 us
    dot_general x18, matrix products, spatial_taps(): jnp.einsum('fhwc,cd->fhwd', padded[:, shift_y:shift_y + rows, shift_x:shi...  47.7 us
    ppermute x4, waiting for transfers between devices, extended(): after = lax.ppermute(first, axis, down)  22.2 us
    ppermute x4, waiting for transfers between devices, extended(): before = lax.ppermute(last, axis, up)  22.2 us
    ppermute x4, starting transfers between devices, extended(): before = lax.ppermute(last, axis, up)  16.8 us
  transfers between devices with their start and end apart: 8, of which 5 were waited for; matrix products, arithmetic and copies ran while one was open for 4% of the time, Pallas kernels for 0%

commit v1 on v0

--- a/solution.py
+++ b/solution.py
@@ -1,6 +1,10 @@
+import functools
+
 import jax
 import jax.numpy as jnp
 from jax import lax
+from jax.experimental import pallas as pl
+from jax.experimental.pallas import tpu as pltpu
 from jax.sharding import PartitionSpec as P
 
 GROUPS = 32
@@ -8,6 +12,7 @@
 
 EPS = 1e-05
 HIGH = lax.Precision.HIGHEST
+MESH = pl.DeviceIdType.MESH
 
 
 def extended(shard, sides, width):
@@ -23,15 +28,65 @@
     return shard
 
 
-def group_moments(value):
+def combine_kernel(n, x_ref, o_ref, slots, send_sem, recv_sem):
+    f, r = lax.axis_index("frame"), lax.axis_index("row")
+    barrier = pltpu.get_barrier_semaphore()
+    for d in range(1, 16):
+        pl.semaphore_signal(barrier, inc=1, device_id=(f, lax.rem(r + d, 16)), device_id_type=MESH)
+        pl.semaphore_signal(barrier, inc=1, device_id=(lax.rem(f + d, 16), r), device_id_type=MESH)
+    pl.semaphore_wait(barrier, 30)
+    tile = x_ref[...]
+    for phase in range(2):
+        me = r if phase == 0 else f
+        s = slots.at[phase]
+        s[me] = tile
+        for d in range(1, 16):
+            to = lax.rem(me + d, 16)
+            pltpu.make_async_remote_copy(
+                s.at[me],
+                s.at[me],
+                send_sem.at[phase],
+                recv_sem.at[phase],
+                device_id=(f, to) if phase == 0 else (to, r),
+                device_id_type=MESH,
+            ).start()
+        pltpu.make_async_copy(s.at[pl.ds(0, 15)], s.at[pl.ds(0, 15)], recv_sem.at[phase]).wait()
+        pltpu.make_async_copy(s.at[pl.ds(0, 15)], s.at[pl.ds(0, 15)], send_sem.at[phase]).wait()
+        v = s[...]
+        means = v[:, 0:1, :]
+        mean = jnp.sum(means, axis=0, keepdims=True) * (1.0 / 16)
+        dev = jnp.sum(v[:, 1:2, :] + (n * 16**phase) * jnp.square(means - mean), axis=0)
+        at = lax.broadcasted_iota(jnp.int32, (8, 128), 0)
+        tile = jnp.where(at == 0, mean[0], jnp.where(at == 1, dev, 0.0))
+    o_ref[...] = tile
+
+
+def combine(tile, n, cid):
+    return pl.pallas_call(
+        functools.partial(combine_kernel, float(n)),
+        out_shape=jax.ShapeDtypeStruct((8, 128), jnp.float32),
+        in_specs=[pl.BlockSpec(memory_space=pltpu.VMEM)],
+        out_specs=pl.BlockSpec(memory_space=pltpu.VMEM),
+        scratch_shapes=[
+            pltpu.VMEM((2, 16, 8, 128), jnp.float32),
+            pltpu.SemaphoreType.DMA((2,)),
+            pltpu.SemaphoreType.DMA((2,)),
+        ],
+        compiler_params=pltpu.CompilerParams(collective_id=cid, has_side_effects=True),
+    )(tile)
+
+
+def group_moments(value, cid):
     width = value.shape[-1]
-    grouped = value.reshape(-1, GROUPS, width // GROUPS)
-    count = grouped.shape[0] * grouped.shape[2] * lax.axis_size("frame") * lax.axis_size("row")
-    totals = lax.psum(jnp.sum(grouped, axis=(0, 2)), ("frame", "row"))
-    mean = totals / count
-    centred = grouped - mean[None, :, None]
-    variance = lax.psum(jnp.sum(centred * centred, axis=(0, 2)), ("frame", "row")) / count
-    return (mean, variance)
+    positions = value.size // width
+    n = positions * (width // GROUPS)
+    sums = jnp.sum(value, axis=(0, 1, 2)).reshape(GROUPS, -1).sum(1)
+    mean = sums / n
+    centred = value - jnp.repeat(mean, width // GROUPS)
+    dev = jnp.sum(centred * centred, axis=(0, 1, 2)).reshape(GROUPS, -1).sum(1)
+    tile = jnp.zeros((8, 128), jnp.float32).at[0, :GROUPS].set(mean).at[1, :GROUPS].set(dev)
+    tile = combine(tile, n, cid)
+    return tile[0, :GROUPS], tile[1, :GROUPS] / (n * lax.axis_size("frame") * lax.axis_size("row"))
 
 
 def activate(value, mean, variance, gain, shift):
@@ -70,18 +125,18 @@
 
 def local(latents, hint, norm_gains, norm_shifts, spatial_kernels, temporal_kernels, zero_weight):
     control_in = latents + hint
-    mean, variance = group_moments(control_in)
+    mean, variance = group_moments(control_in, 1)
     active = activate(control_in, mean, variance, norm_gains[0], norm_shifts[0])
     inner = spatial_taps(extended(active, (("row", 1),), 1), spatial_kernels[0])
-    mean, variance = group_moments(inner)
+    mean, variance = group_moments(inner, 2)
     active = activate(inner, mean, variance, norm_gains[1], norm_shifts[1])
     control_out = control_in + temporal(active, temporal_kernels[0])
     skip = latents + jnp.einsum("fhwc,cd->fhwd", control_out, zero_weight, precision=HIGH)
-    mean, variance = group_moments(skip)
+    mean, variance = group_moments(skip, 3)
     middle = activate(skip, mean, variance, norm_gains[2], norm_shifts[2])
     padded = extended(middle, (("row", 1),), 1)
     inner = spatial_taps(padded, spatial_kernels[1])
-    mean, variance = group_moments(inner)
+    mean, variance = group_moments(inner, 4)
     active = activate(inner, mean, variance, norm_gains[3], norm_shifts[3])
     return skip + temporal(active, temporal_kernels[1])
 

time: 779 us -> 257 us (0.33)
  the two profiles are of different devices: /device:TPU:1 before, /device:TPU:32 now
where the time goes in v1:
time: 257 us; the launch traced here: 252 us
  Pallas kernels  77.2 us (30%)
  matrix products  70 us (27%)
  waiting for transfers between devices  40.6 us (16%)
  local copies, waits for them, and re-layouts  29.4 us (11%)
  starting transfers between devices  21 us (8%)
  other arithmetic  13.1 us (5%)
    pallas_call x4, Pallas kernels, combine(): pl.pallas_call(functools.partial(combine_kernel, float(n)), out_shape=jax...  77.2 us
    dot_general x18, matrix products, spatial_taps(): jnp.einsum('fhwc,cd->fhwd', padded[:, shift_y:shift_y + rows, shift_x:shi...  48.4 us
    ppermute x4, waiting for transfers between devices, extended(): after = lax.ppermute(first, axis, down)  40.6 us
    dot_general x6, matrix products, temporal(): jnp.einsum('fhwc,cd->fhwd', padded[tap:tap + frames], kernel[tap], precis...  19.1 us
    unnamed x30, local copies, waits for them, and re-layouts  15.3 us
    ppermute x4, starting transfers between devices, extended(): after = lax.ppermute(first, axis, down)  11.3 us
    ppermute x4, starting transfers between devices, extended(): before = lax.ppermute(last, axis, up)  9.72 us
    slice x1, local copies, waits for them, and re-layouts, local(): inner = spatial_taps(padded, spatial_kernels[1])  7.77 us
  transfers between devices with their start and end apart: 8, of which 2 were waited for; matrix products, arithmetic and copies ran while one was open for 16% of the time, Pallas kernels for 0%

profile of v1, /device:TPU:32, one launch (start us, length us, event | category | flops | bytes accessed | tf_op | source)
XLA Modules:
  0.0 252.4 jit_solution(858619269200313882)
XLA Ops:
  0.0 2.0 fusion.112
  2.4 0.3 multiply_reduce_fusion.3
  3.2 0.6 copy-done.7
  3.8 20.2 %shard_map.73 = f32[8,128]{1,0:T(8,128)} custom-call(f32[8,128]{1,0:T(8,128)} %copy-done.7), custom_call_target="tpu_custom_call" | custom-call | tf_op jit(solution)/shard_map/pallas_call | solution.py:65
  24.0 0.8 slice_bitcast_fusion.39
  25.2 0.6 divide_multiply_fusion.3
  25.8 0.9 fusion.117
  26.7 2.0 collective-permute-start
  28.7 1.3 collective-permute-start.1
  30.0 7.8 %fusion.113 = (f32[1,3,3,320,320]{4,3,2,1,0:T(8,128)}, f32[1,3,3,320,320]{4,3,2,1,0:T(8,128)}) fusion(f32[2,3,3,320,320]{4,3,2,1,0:T(8,128)} %param.27), kind=kLoop, calls=%fused_computation.158 | loop fusion | bytes 14745600 | tf_op jit(solution)/shard_map/slice | solution.py:138
  37.8 6.5 %copy.46 = f32[1,3,3,320,320]{3,4,2,1,0:T(8,128)} copy(f32[1,3,3,320,320]{4,3,2,1,0:T(8,128)} %get-tuple-element.112) | data formatting | bytes 7372800
  44.2 3.5 %fusion.84 = f32[2,4,112,320]{2,3,1,0:T(8,128)S(1)} fusion(f32[2,4,112,320]{2,3,1,0:T(8,128)S(1)} %divide_multiply_fusion.3, f32[3,3,320,320]{2,3,1,0:T(8,128)} %bitcast.226), kind=kOutput, calls=%fused_computation.105 | convolution fusion | flops 1101004800 | bytes 2785280 | tf_op jit(solution)/shard_map/fhwc,cd->fhwd/dot_general | solution.py:106
  47.7 1.6 select_maximum_fusion.2
  49.3 2.3 fusion.78
  51.6 2.5 fusion.80
  54.1 2.5 fusion.73
  56.5 2.3 fusion.75
  58.8 3.5 %fusion.17 = f32[2,4,112,320]{2,3,1,0:T(8,128)S(1)} fusion(f32[2,4,112,320]{2,3,1,0:T(8,128)S(1)} %divide_multiply_fusion.3, f32[2,1,112,320]{2,3,1,0:T(8,128)} %collective-permute-done, f32[3,3,320,320]{2,3,1,0:T(8,128)S(1)} %bitcast.231), kind=kOutput, calls=%fused_computation.23 | convolution fusion | flops 1101363200 | bytes 3235840 | tf_op jit(solution)/shard_map/fhwc,cd->fhwd/dot_general | solution.py:106
  62.4 2.5 fusion.47
  64.9 2.3 fusion.21
  67.2 2.9 %fusion.118 = (f32[320]{0:T(512)S(1)}, f32[2,4,112,320]{2,3,1,0:T(8,128)S(1)}) fusion(f32[2,4,112,320]{2,3,1,0:T(8,128)S(1)} %fusion.73, f32[2,4,112,320]{2,3,1,0:T(8,128)S(1)} %fusion.21, f32[2,4,112,320]{2,3,1,0:T(8,128)S(1)} %fusion.75, f32[2,4,112,320]{2,3,1,0:T(8,128)S(1)} %fusion.47, f32[3,3,320,320]{2,3,1,0:T(8,128)S(1)} %bitcast.234, ...), kind=kOutput, calls=%fused_computation.163 | convolution fusion | flops 1102438144 | bytes 8193280 | tf_op jit(solution)/shard_map/fhwc,cd->fhwd/dot_general | solution.py:106
  70.5 0.3 multiply_reduce_fusion.2
  71.3 0.6 copy-done.8
  71.9 19.4 %shard_map.74 = f32[8,128]{1,0:T(8,128)} custom-call(f32[8,128]{1,0:T(8,128)} %copy-done.8), custom_call_target="tpu_custom_call" | custom-call | tf_op jit(solution)/shard_map/pallas_call | solution.py:65
  91.3 0.7 slice_bitcast_fusion.38
  92.4 1.9 divide_multiply_fusion.2
  94.3 1.2 fusion.116
  95.5 4.0 %collective-permute-start.3 = (f32[1,4,112,320]{2,3,1,0:T(8,128)}, f32[1,4,112,320]{2,3,1,0:T(8,128)}, u32[]{:S(2)}, u32[]{:S(2)}) collective-permute-start(f32[1,4,112,320]{2,3,1,0:T(8,128)} %get-tuple-element.118), channel_id=1, source_target_pairs={{16,0},{32,16},{48,32},{64,48},{80,64},{96,80},{112,96},{128,112},... | collective-permute-start | bytes 1720328 | tf_op jit(solution)/shard_map/ppermute | solution.py:26
  99.5 3.3 %collective-permute-start.2 = (f32[1,4,112,320]{2,3,1,0:T(8,128)}, f32[1,4,112,320]{2,3,1,0:T(8,128)}, u32[]{:S(2)}, u32[]{:S(2)}) collective-permute-start(f32[1,4,112,320]{2,3,1,0:T(8,128)} %get-tuple-element.117), channel_id=1, source_target_pairs={{0,16},{16,32},{32,48},{48,64},{64,80},{80,96},{96,112},{112,128},... | collective-permute-start | bytes 1720328 | tf_op jit(solution)/shard_map/ppermute | solution.py:25
  102.9 6.5 %copy.47 = f32[1,3,3,320,320]{3,4,2,1,0:T(8,128)} copy(f32[1,3,3,320,320]{4,3,2,1,0:T(8,128)} %get-tuple-element.111) | data formatting | bytes 7372800
  109.3 3.3 %fusion.90 = f32[2,4,112,320]{2,3,1,0:T(8,128)S(1)} fusion(f32[2,4,112,320]{2,3,1,0:T(8,128)S(1)} %divide_multiply_fusion.2, f32[2,3,320,320]{3,2,1,0:T(8,128)} %param.28), kind=kOutput, calls=%fused_computation.115 | convolution fusion | flops 1101004800 | bytes 2785280 | tf_op jit(solution)/shard_map/fhwc,cd->fhwd/dot_general | solution.py:120
  112.7 16.7 %collective-permute-done.3 = f32[1,4,112,320]{2,3,1,0:T(8,128)} collective-permute-done((f32[1,4,112,320]{2,3,1,0:T(8,128)}, f32[1,4,112,320]{2,3,1,0:T(8,128)}, u32[]{:S(2)}, u32[]{:S(2)}) %collective-permute-start.3) | collective-permute-done | bytes 573472 | tf_op jit(solution)/shard_map/ppermute | solution.py:26
  129.4 3.6 %fusion.4 = f32[2,4,112,320]{2,3,1,0:T(8,128)S(1)} fusion(f32[1,4,112,320]{2,3,1,0:T(8,128)} %collective-permute-done.3, f32[2,4,112,320]{2,3,1,0:T(8,128)S(1)} %divide_multiply_fusion.2, f32[2,3,320,320]{3,2,1,0:T(8,128)} %param.28), kind=kOutput, calls=%fused_computation.10 | convolution fusion | flops 1101434880 | bytes 3440640 | tf_op jit(solution)/shard_map/fhwc,cd->fhwd/dot_general | solution.py:120
  133.0 3.9 %fusion.57 = f32[2,4,112,320]{2,3,1,0:T(8,128)S(1)} fusion(f32[2,4,112,320]{2,3,1,0:T(8,128)S(1)} %get-tuple-element.110, f32[2,4,112,320]{2,3,1,0:T(8,128)S(1)} %fusion.4, f32[2,4,112,320]{2,3,1,0:T(8,128)S(1)} %fusion.90, f32[2,4,112,320]{2,3,1,0:T(8,128)S(1)} %divide_multiply_fusion.2, f32[1,4,112,320]{2,3,1,0:T(8,128)} %collective-permute-done.2, ...), kind=kOutput, calls=%fused_computation.60 | convolution fusion | flops 1102295040 | bytes 6881280 | tf_op jit(solution)/shard_map/fhwc,cd->fhwd/dot_general | solution.py:120
  136.9 2.5 fusion.119
  139.8 0.3 multiply_reduce_fusion.1
  140.5 0.6 copy-done.9
  141.1 15.4 %shard_map.75 = f32[8,128]{1,0:T(8,128)} custom-call(f32[8,128]{1,0:T(8,128)} %copy-done.9), custom_call_target="tpu_custom_call" | custom-call | tf_op jit(solution)/shard_map/pallas_call | solution.py:65
  156.6 0.8 slice_bitcast_fusion.37
  157.7 0.6 divide_multiply_fusion.1
  158.4 1.4 collective-permute-start.4
  159.8 1.5 collective-permute-start.5
  161.3 3.4 %fusion.83 = f32[2,4,112,320]{2,3,1,0:T(8,128)S(1)} fusion(f32[2,4,112,320]{2,3,1,0:T(8,128)S(1)} %divide_multiply_fusion.1, f32[3,3,320,320]{2,3,1,0:T(8,128)} %bitcast.215), kind=kOutput, calls=%fused_computation.95 | convolution fusion | flops 1101004800 | bytes 2785280 | tf_op jit(solution)/shard_map/fhwc,cd->fhwd/dot_general | solution.py:106
  164.7 0.6 select_maximum_fusion
  165.3 3.5 %fusion.70 = f32[2,4,112,320]{2,3,1,0:T(8,128)S(1)} fusion(f32[2,6,114,320]{2,3,1,0:T(8,128)S(1)} %select_maximum_fusion, f32[3,3,320,320]{2,3,1,0:T(8,128)} %bitcast.216), kind=kOutput, calls=%fused_computation.69 | convolution fusion | flops 1101004800 | bytes 2949120 | tf_op jit(solution)/shard_map/fhwc,cd->fhwd/dot_general | solution.py:106
  168.8 2.3 fusion.68
  171.1 2.3 fusion.65
  173.4 2.7 %fusion.63 = f32[2,4,112,320]{2,3,1,0:T(8,128)S(1)} fusion(f32[2,6,114,320]{2,3,1,0:T(8,128)S(1)} %select_maximum_fusion, f32[3,3,320,320]{2,3,1,0:T(8,128)S(1)} %bitcast.221), kind=kOutput, calls=%fused_computation.62 | convolution fusion | flops 1101004800 | bytes 2949120 | tf_op jit(solution)/shard_map/fhwc,cd->fhwd/dot_general | solution.py:106
  176.1 2.3 fusion.25
  178.4 2.5 fusion.53
  181.0 2.3 fusion.29
  183.3 2.9 %fusion.120 = (f32[320]{0:T(512)S(1)}, f32[2,4,112,320]{2,3,1,0:T(8,128)S(1)}) fusion(f32[2,4,112,320]{2,3,1,0:T(8,128)S(1)} %fusion.63, f32[2,4,112,320]{2,3,1,0:T(8,128)S(1)} %fusion.29, f32[2,4,112,320]{2,3,1,0:T(8,128)S(1)} %fusion.65, f32[2,4,112,320]{2,3,1,0:T(8,128)S(1)} %fusion.53, f32[3,3,320,320]{2,3,1,0:T(8,128)S(1)} %bitcast.225, ...), kind=kOutput, calls=%fused_computation.165 | convolution fusion | flops 1102438144 | bytes 8193280 | tf_op jit(solution)/shard_map/fhwc,cd->fhwd/dot_general | solution.py:106
  186.6 0.3 multiply_reduce_fusion
  187.2 0.4 scatter.39.x_ref
  187.7 0.6 copy-done.6
  188.2 22.3 %shard_map.76 = f32[8,128]{1,0:T(8,128)} custom-call(f32[8,128]{1,0:T(8,128)} %copy-done.6), custom_call_target="tpu_custom_call" | custom-call | tf_op jit(solution)/shard_map/pallas_call | solution.py:65
  210.5 0.8 slice_bitcast_fusion.36
  211.7 0.6 divide_multiply_fusion
  212.4 4.6 %collective-permute-start.7 = (f32[1,4,112,320]{2,3,1,0:T(8,128)S(1)}, f32[1,4,112,320]{2,3,1,0:T(8,128)S(1)}, u32[]{:S(2)}, u32[]{:S(2)}) collective-permute-start(f32[1,4,112,320]{2,3,1,0:T(8,128)S(1)} %get-tuple-element.114), channel_id=1, source_target_pairs={{16,0},{32,16},{48,32},{64,48},{80,64},{96,80},{112,96},{128,112},... | collective-permute-start | bytes 1720328 | tf_op jit(solution)/shard_map/ppermute | solution.py:26
  217.0 2.9 %collective-permute-start.6 = (f32[1,4,112,320]{2,3,1,0:T(8,128)S(1)}, f32[1,4,112,320]{2,3,1,0:T(8,128)S(1)}, u32[]{:S(2)}, u32[]{:S(2)}) collective-permute-start(f32[1,4,112,320]{2,3,1,0:T(8,128)S(1)} %get-tuple-element.113), channel_id=1, source_target_pairs={{0,16},{16,32},{32,48},{48,64},{64,80},{80,96},{96,112},{112,128},... | collective-permute-start | bytes 1720328 | tf_op jit(solution)/shard_map/ppermute | solution.py:25
  219.9 2.3 fusion.86
  222.2 23.9 %collective-permute-done.7 = f32[1,4,112,320]{2,3,1,0:T(8,128)S(1)} collective-permute-done((f32[1,4,112,320]{2,3,1,0:T(8,128)S(1)}, f32[1,4,112,320]{2,3,1,0:T(8,128)S(1)}, u32[]{:S(2)}, u32[]{:S(2)}) %collective-permute-start.7) | collective-permute-done | bytes 573472 | tf_op jit(solution)/shard_map/ppermute | solution.py:26
  246.1 2.4 fusion.12
  248.5 3.6 %fusion.60 = f32[2,4,112,320]{2,3,1,0:T(8,128)} fusion(f32[2,4,112,320]{2,3,1,0:T(8,128)S(1)} %get-tuple-element.140, f32[2,4,112,320]{2,3,1,0:T(8,128)S(1)} %fusion.12, f32[2,4,112,320]{2,3,1,0:T(8,128)S(1)} %fusion.86, f32[2,4,112,320]{2,3,1,0:T(8,128)S(1)} %divide_multiply_fusion, f32[1,4,112,320]{2,3,1,0:T(8,128)S(1)} %collective-permute-done.6, ...), kind=kOutput, calls=%fused_computation.61 | convolution fusion | flops 1102295040 | bytes 7536640 | tf_op jit(solution)/shard_map/fhwc,cd->fhwd/dot_general | solution.py:120
  (85 shorter events, 4.8 us)
Async XLA Ops:
  0.0 136.8 %copy-start = (f32[320,320]{1,0:T(8,128)S(1)}, f32[320,320]{1,0:T(8,128)}, u32[]{:S(2)}) copy-start(f32[320,320]{1,0:T(8,128)} %param.29) | copy-start | bytes 1228804
  2.0 23.1 %copy-start.10 = (f32[4,320]{1,0:T(4,128)S(1)}, f32[4,320]{1,0:T(4,128)}, u32[]{:S(2)}) copy-start(f32[4,320]{1,0:T(4,128)} %param.26) | copy-start | bytes 15364
  2.0 23.1 %copy-start.11 = (f32[4,320]{1,0:T(4,128)S(1)}, f32[4,320]{1,0:T(4,128)}, u32[]{:S(2)}) copy-start(f32[4,320]{1,0:T(4,128)} %param.25) | copy-start | bytes 15364
  3.2 0.6 copy-start.7
  26.7 21.1 %collective-permute-start = (f32[2,1,112,320]{2,3,1,0:T(8,128)}, f32[2,1,112,320]{2,3,1,0:T(8,128)}, u32[]{:S(2)}, u32[]{:S(2)}) collective-permute-start(f32[2,1,112,320]{2,3,1,0:T(8,128)} %get-tuple-element.119), channel_id=1, source_target_pairs={{0,1},{1,2},{2,3},{3,4},{4,5},{5,6},{6,7},{7,8},{8,9},{9,10},{10,1... | collective-permute-start | bytes 860168 | tf_op jit(solution)/shard_map/ppermute | solution.py:25
  28.7 19.0 %collective-permute-start.1 = (f32[2,1,112,320]{2,3,1,0:T(8,128)}, f32[2,1,112,320]{2,3,1,0:T(8,128)S(1)}, u32[]{:S(2)}, u32[]{:S(2)}) collective-permute-start(f32[2,1,112,320]{2,3,1,0:T(8,128)} %get-tuple-element.120), channel_id=1, source_target_pairs={{1,0},{2,1},{3,2},{4,3},{5,4},{6,5},{7,6},{8,7},{9,8},{10,9},{11,1... | collective-permute-start | bytes 860168 | tf_op jit(solution)/shard_map/ppermute | solution.py:26
  44.2 5.1 %copy-start.2 = (f32[1,3,3,320,320]{3,4,2,1,0:T(8,128)S(1)}, f32[1,3,3,320,320]{3,4,2,1,0:T(8,128)}, u32[]{:S(2)}) copy-start(f32[1,3,3,320,320]{3,4,2,1,0:T(8,128)} %copy.46) | copy-start | bytes 11059204
  70.1 22.3 %copy-start.3 = (f32[2,4,112,320]{2,3,1,0:T(8,128)}, f32[2,4,112,320]{2,3,1,0:T(8,128)S(1)}, u32[]{:S(2)}) copy-start(f32[2,4,112,320]{2,3,1,0:T(8,128)S(1)} %get-tuple-element.138) | copy-start | bytes 3440644
  71.3 0.6 copy-start.8
  95.5 33.8 %collective-permute-start.3 = (f32[1,4,112,320]{2,3,1,0:T(8,128)}, f32[1,4,112,320]{2,3,1,0:T(8,128)}, u32[]{:S(2)}, u32[]{:S(2)}) collective-permute-start(f32[1,4,112,320]{2,3,1,0:T(8,128)} %get-tuple-element.118), channel_id=1, source_target_pairs={{16,0},{32,16},{48,32},{64,48},{80,64},{96,80},{112,96},{128,112},... | collective-permute-start | bytes 1720328 | tf_op jit(solution)/shard_map/ppermute | solution.py:26
  99.5 33.4 %collective-permute-start.2 = (f32[1,4,112,320]{2,3,1,0:T(8,128)}, f32[1,4,112,320]{2,3,1,0:T(8,128)}, u32[]{:S(2)}, u32[]{:S(2)}) collective-permute-start(f32[1,4,112,320]{2,3,1,0:T(8,128)} %get-tuple-element.117), channel_id=1, source_target_pairs={{0,16},{16,32},{32,48},{48,64},{64,80},{80,96},{96,112},{112,128},... | collective-permute-start | bytes 1720328 | tf_op jit(solution)/shard_map/ppermute | solution.py:25
  132.9 3.9 %copy-start.4 = (f32[2,4,112,320]{2,3,1,0:T(8,128)S(1)}, f32[2,4,112,320]{2,3,1,0:T(8,128)}, u32[]{:S(2)}) copy-start(f32[2,4,112,320]{2,3,1,0:T(8,128)} %param.23) | copy-start | bytes 3440644
  140.5 0.6 copy-start.9
  157.7 11.1 %slice-start = ((s8[4423680]{0:T(1024)(128)(4,1)}), s8[4194304]{0:T(1024)(128)(4,1)S(1)}, s32[]{:S(2)}) async-start(s8[4423680]{0:T(1024)(128)(4,1)} %bitcast.217), calls=%async_computation | async-start | bytes 8388608
  158.4 6.3 %collective-permute-start.4 = (f32[2,1,112,320]{2,3,1,0:T(8,128)S(1)}, f32[2,1,112,320]{2,3,1,0:T(8,128)S(1)}, u32[]{:S(2)}, u32[]{:S(2)}) collective-permute-start(f32[2,1,112,320]{2,3,1,0:T(8,128)S(1)} %get-tuple-element.115), channel_id=1, source_target_pairs={{0,1},{1,2},{2,3},{3,4},{4,5},{5,6},{6,7},{7,8},{8,9},{9,10},{10,1... | collective-permute-start | bytes 860168 | tf_op jit(solution)/shard_map/ppermute | solution.py:25
  159.8 4.9 %collective-permute-start.5 = (f32[2,1,112,320]{2,3,1,0:T(8,128)S(1)}, f32[2,1,112,320]{2,3,1,0:T(8,128)S(1)}, u32[]{:S(2)}, u32[]{:S(2)}) collective-permute-start(f32[2,1,112,320]{2,3,1,0:T(8,128)S(1)} %get-tuple-element.116), channel_id=1, source_target_pairs={{1,0},{2,1},{3,2},{4,3},{5,4},{6,5},{7,6},{8,7},{9,8},{10,9},{11,1... | collective-permute-start | bytes 860168 | tf_op jit(solution)/shard_map/ppermute | solution.py:26
  161.3 7.5 %slice-start.1 = ((s8[4423680]{0:T(1024)(128)(4,1)}), s8[229376]{0:T(1024)(128)(4,1)S(1)}, s32[]{:S(2)}) async-start(s8[4423680]{0:T(1024)(128)(4,1)} %bitcast.217), calls=%async_computation.1 | async-start | bytes 458752
  187.6 0.6 copy-start.6
  211.7 8.2 %copy-start.5 = (f32[2,3,320,320]{3,2,1,0:T(8,128)S(1)}, f32[2,3,320,320]{3,2,1,0:T(8,128)}, u32[]{:S(2)}) copy-start(f32[2,3,320,320]{3,2,1,0:T(8,128)} %param.28) | copy-start | bytes 7372804
  212.4 33.8 %collective-permute-start.7 = (f32[1,4,112,320]{2,3,1,0:T(8,128)S(1)}, f32[1,4,112,320]{2,3,1,0:T(8,128)S(1)}, u32[]{:S(2)}, u32[]{:S(2)}) collective-permute-start(f32[1,4,112,320]{2,3,1,0:T(8,128)S(1)} %get-tuple-element.114), channel_id=1, source_target_pairs={{16,0},{32,16},{48,32},{64,48},{80,64},{96,80},{112,96},{128,112},... | collective-permute-start | bytes 1720328 | tf_op jit(solution)/shard_map/ppermute | solution.py:26
  217.0 31.5 %collective-permute-start.6 = (f32[1,4,112,320]{2,3,1,0:T(8,128)S(1)}, f32[1,4,112,320]{2,3,1,0:T(8,128)S(1)}, u32[]{:S(2)}, u32[]{:S(2)}) collective-permute-start(f32[1,4,112,320]{2,3,1,0:T(8,128)S(1)} %get-tuple-element.113), channel_id=1, source_target_pairs={{0,16},{16,32},{32,48},{48,64},{64,80},{80,96},{96,112},{112,128},... | collective-permute-start | bytes 1720328 | tf_op jit(solution)/shard_map/ppermute | solution.py:25
  248.5 3.6 %copy-start.1 = (f32[320,320]{1,0:T(8,128)S(1)}, f32[320,320]{1,0:T(8,128)}, u32[]{:S(2)}) copy-start(f32[320,320]{1,0:T(8,128)} %param.29) | copy-start | bytes 1228804

commit v2 on v0

v2 whole, which is shorter than its diff:
```python
import functools

import jax
import jax.numpy as jnp
from jax import lax
from jax.experimental import pallas as pl
from jax.experimental.pallas import tpu as pltpu
from jax.sharding import PartitionSpec as P

EPS = 1e-05
MESH = pl.DeviceIdType.MESH
F32, BF16 = jnp.float32, jnp.bfloat16
C = 320
W = 112
L = 128
PER = 10
K = 3 * C
ROW_LOCAL = 2 * 4 * W * PER

FARHALO, FAR, NEAR, NEARHALO = range(4)


def split(v):
    hi = v.astype(BF16)
    return hi, (v - hi.astype(F32)).astype(BF16)


def kernel(
    lat_ref, hint_ref, gain_ref, shift_ref, sk_hbm, tk_hbm, zw_hbm, out_ref,
    ci, skip, inner, act, tact, wst, wsp, wtm, wz, cols, const, slots,
    wsem, ar_s, ar_r, row_s, row_r, near_s, near_r, far_s, far_r,
):
    f, r = lax.axis_index("frame"), lax.axis_index("row")
    odd = lax.rem(f, 2)
    partner = f + 1 - 2 * odd
    outer = lax.rem(f + 15 + 2 * odd, 16)
    above, below = lax.rem(r + 15, 16), lax.rem(r + 1, 16)
    has_far = jnp.where(odd == 0, f > 0, f < 15)
    far_at, near_at = odd, 1 - odd

    barrier = pltpu.get_barrier_semaphore()
    for d in range(1, 16):
        pl.semaphore_signal(barrier, inc=1, device_id=(f, lax.rem(r + d, 16)), device_id_type=MESH)
        pl.semaphore_signal(barrier, inc=1, device_id=(lax.rem(f + d, 16), r), device_id_type=MESH)

    weight_copies = []
    for j in range(2):
        for dy in range(3):
            for dx in range(3):
                i = j * 9 + dy * 3 + dx
                weight_copies.append(pltpu.make_async_copy(sk_hbm.at[j, dy, dx], wst.at[i], wsem.at[i]))
    for j in range(2):
        for t in range(3):
            i = 18 + j * 3 + t
            tap = t + odd * (2 - 2 * t)
            weight_copies.append(pltpu.make_async_copy(tk_hbm.at[j, tap], wst.at[i], wsem.at[i]))
    weight_copies.append(pltpu.make_async_copy(zw_hbm, wst.at[24], wsem.at[24]))
    order = list(range(9)) + [18, 19, 20, 24] + list(range(9, 18)) + [21, 22, 23]
    for i in order:
        weight_copies[i].start()

    lane = lax.broadcasted_iota(jnp.int32, (C, L), 1)
    channel = lax.broadcasted_iota(jnp.int32, (C, L), 0)
    inside = lane < W
    member = jnp.where((channel >= PER * lane) & (channel < PER * lane + PER), 1.0, 0.0).astype(F32)

    def to_groups(col):
        return jnp.sum(col * member, axis=0, keepdims=True)

    def to_channels(row):
        return jnp.sum(row * member, axis=1, keepdims=True)

    def eye(dtype):
        a = lax.broadcasted_iota(jnp.int32, (C, C), 0)
        b = lax.broadcasted_iota(jnp.int32, (C, C), 1)
        return jnp.where(a == b, 1.0, 0.0).astype(dtype)

    for slot, at in ((0, far_at), (1, near_at)):
        for i in range(4):
            ci[slot, 1 + i] = jnp.zeros((C, L), F32)
            skip[slot, 1 + i] = jnp.zeros((C, L), F32)
            v = lat_ref[at, i]
            skip[slot, 1 + i, :, 0:W] = v
            ci[slot, 1 + i, :, 0:W] = v + hint_ref[at, i]

    def local_tile(read):
        total = lax.fori_loop(0, 8, lambda i, a: a + read(i // 4, lax.rem(i, 4)), jnp.zeros((C, L), F32))
        mean = to_groups(jnp.sum(total, axis=1, keepdims=True)) * (1.0 / ROW_LOCAL)
        col = to_channels(mean)

        def squares(i, a):
            c = jnp.where(inside, read(i // 4, lax.rem(i, 4)) - col, 0.0)
            return a + c * c

        dev = to_groups(jnp.sum(lax.fori_loop(0, 8, squares, jnp.zeros((C, L), F32)), axis=1, keepdims=True))
        return pack(mean, dev)

    def pack(mean, dev):
        at = lax.broadcasted_iota(jnp.int32, (8, L), 0)
        return jnp.where(at == 0, mean, jnp.where(at == 1, dev, 0.0))

    def ar_send(k, phase, tile):
        me = r if phase == 0 else f
        s = slots.at[k, phase]
        s[me] = tile
        for d in range(1, 16):
            to = lax.rem(me + d, 16)
            pltpu.make_async_remote_copy(
                s.at[me], s.at[me], ar_s.at[k, phase], ar_r.at[k, phase],
                device_id=(f, to) if phase == 0 else (to, r), device_id_type=MESH,
            ).start()

    def ar_wait(k, phase):
        s = slots.at[k, phase]
        pltpu.make_async_copy(s.at[pl.ds(0, 15)], s.at[pl.ds(0, 15)], ar_r.at[k, phase]).wait()
        v = s[...]
        means = v[:, 0:1, :]
        mean = jnp.sum(means, axis=0, keepdims=True) * (1.0 / 16)
        dev = jnp.sum(v[:, 1:2, :] + (ROW_LOCAL * 16.0**phase) * jnp.square(means - mean), axis=0)
        return mean[0], dev

    def set_const(k, mean, dev):
        rstd = lax.rsqrt(dev * (1.0 / (256.0 * ROW_LOCAL)) + EPS)
        const[0] = jnp.broadcast_to(to_channels(mean), (C, L))
        const[1] = to_channels(rstd) * cols[2 * k]
        const[2] = cols[2 * k + 1]

    def activated(v, ok):
        u = (v - const[0]) * const[1] + const[2]
        return split(jnp.where(inside & ok, u / (1.0 + jnp.exp(-u)), 0.0))

    def remote(src, dst, sends, recvs, at, device):
        return pltpu.make_async_remote_copy(
            src, dst, sends.at[at], recvs.at[at], device_id=device, device_id_type=MESH
        )

    started = []

    def edge_copies(block, buf, slot):
        return [
            remote(buf.at[slot, 4], buf.at[slot, 0], row_s, row_r, block * 6 + slot * 2, (f, below)),
            remote(buf.at[slot, 1], buf.at[slot, 5], row_s, row_r, block * 6 + slot * 2 + 1, (f, above)),
        ]

    def near_copies(block, buf):
        dev = (partner, r)
        return [
            remote(buf.at[1, 1], buf.at[2, 1], near_s, near_r, block * 3, dev),
            remote(buf.at[1, 4], buf.at[2, 4], near_s, near_r, block * 3 + 1, dev),
            remote(buf.at[1, pl.ds(2, 2)], buf.at[2, pl.ds(2, 2)], near_s, near_r, block * 3 + 2, dev),
        ]

    def far_copy(block, j):
        return remote(
            inner.at[block, FAR, pl.ds(2 * j, 2)], inner.at[block, FARHALO, pl.ds(2 * j, 2)],
            far_s, far_r, block * 2 + j, (outer, r),
        )

    def start(copies):
        for c in copies:
            c.start()
            started.append(c)

    def prep_spatial(j, dx):
        parts = []
        for dy in range(3):
            weight_copies[j * 9 + dy * 3 + dx].wait()
            hi, lo = split(wst[j * 9 + dy * 3 + dx])
            parts += [hi, hi, lo]
        t = lax.dot_general(
            eye(BF16), jnp.concatenate(parts, axis=0), (((1,), (1,)), ((), ())), preferred_element_type=F32
        )
        wsp[j, dx * C : (dx + 1) * C, :] = t.astype(BF16)

    def prep_small(dst, which):
        parts = []
        for i in which:
            weight_copies[i].wait()
            hi, lo = split(wst[i])
            parts += [hi, hi, lo]
        t = lax.dot_general(
            eye(BF16), jnp.concatenate(parts, axis=0), (((1,), (1,)), ((), ())), preferred_element_type=F32
        )
        dst[...] = t.astype(BF16)

    def act_frame(buf, slot):
        def body(i, _):
            ok = ((i > 0) | (r > 0)) & ((i < 5) | (r < 15))
            hi, lo = activated(buf[slot, i], ok)
            at = pl.ds(pl.multiple_of(i * L, L), L)
            act[slot, 0:C, at] = hi
            act[slot, C : 2 * C, at] = lo
            act[slot, 2 * C : K, at] = hi
            return 0

        lax.fori_loop(0, 6, body, 0)

    def spatial(block, slot, dst):
        def body(j, _):
            rhs = jnp.concatenate(
                [act[slot, :, pl.ds(pl.multiple_of(j * 2 * L + dy * L, L), 2 * L)] for dy in range(3)], axis=0
            )
            y = jnp.dot(wsp[block], rhs, preferred_element_type=F32)
            for h in range(2):
                part = y[:, h * L : (h + 1) * L]
                o = part[C : 2 * C] + pltpu.roll(part[0:C], 1, 1) + pltpu.roll(part[2 * C : K], L - 1, 1)
                inner[block, dst, 2 * j + h] = jnp.where(inside, o, 0.0)
            if dst == FAR:
                far_copy(block, j).start()
            return 0

        lax.fori_loop(0, 2, body, 0)

    def act_temporal(block, slot, ok):
        def body(i, _):
            hi, lo = activated(inner[block, slot, i], ok)
            at = pl.ds(pl.multiple_of(i * L, L), L)
            tact[slot, 0:C, at] = hi
            tact[slot, C : 2 * C, at] = lo
            tact[slot, 2 * C : K, at] = hi
            return 0

        lax.fori_loop(0, 4, body, 0)

    def temporal(block, own):
        def body(j, _):
            at = pl.ds(pl.multiple_of(j * 2 * L, L), 2 * L)
            rhs = jnp.concatenate([tact[own + t, :, at] for t in range(3)], axis=0)
            y = jnp.dot(wtm[block], rhs, preferred_element_type=F32)
            rows = [1 + 2 * j, 2 + 2 * j]
            if block == 0:
                co = jnp.concatenate([ci[own, rows[0]], ci[own, rows[1]]], axis=1) + y
                hi, lo = split(co)
                z = jnp.dot(wz[...], jnp.concatenate([hi, lo, hi], axis=0), preferred_element_type=F32)
                for h in range(2):
                    skip[own, rows[h]] = skip[own, rows[h]] + jnp.where(inside, z[:, h * L : (h + 1) * L], 0.0)
            else:
                for h in range(2):
                    o = skip[own, rows[h]] + y[:, h * L : (h + 1) * L]
                    out_ref[far_at if own == 0 else near_at, 2 * j + h] = o[:, 0:W]
            return 0

        lax.fori_loop(0, 2, body, 0)

    def gain_columns():
        e = eye(F32)
        for k in range(4):
            for i, src in enumerate((gain_ref, shift_ref)):
                col = jnp.sum(e * src[k : k + 1, :], axis=1, keepdims=True)
                cols[2 * k + i] = jnp.broadcast_to(col, (C, L))

    tile = local_tile(lambda a, i: ci[a, 1 + i])
    pl.semaphore_wait(barrier, 30)

    for block, buf in ((0, ci), (1, skip)):
        ar_send(2 * block, 0, tile)
        edges = [edge_copies(block, buf, slot) for slot in range(3)]
        nears = near_copies(block, buf)
        if block == 0:
            start(nears[:2])
            start(edges[1])
            start(edges[0])
            start(nears[2:])
            gain_columns()
        prep_spatial(block, 0)
        mean, dev = ar_wait(2 * block, 0)
        ar_send(2 * block, 1, pack(mean, dev))
        prep_spatial(block, 1)
        prep_spatial(block, 2)
        nears[0].wait_recv()
        nears[1].wait_recv()
        start(edges[2])
        mean, dev = ar_wait(2 * block, 1)
        set_const(2 * block, mean, dev)
        for slot, dst in ((0, FAR), (1, NEAR)):
            for c in edges[slot]:
                c.wait_recv()
            act_frame(buf, slot)
            spatial(block, slot, dst)
        tile = local_tile(lambda a, i: inner[block, FAR + a, i])
        ar_send(2 * block + 1, 0, tile)
        for c in edges[2]:
            c.wait_recv()
        nears[2].wait_recv()
        act_frame(buf, 2)
        spatial(block, 2, NEARHALO)
        mean, dev = ar_wait(2 * block + 1, 0)
        ar_send(2 * block + 1, 1, pack(mean, dev))
        prep_small(wtm.at[block], [18 + 3 * block + t for t in range(3)])
        if block == 0:
            prep_small(wz, [24])
        mean, dev = ar_wait(2 * block + 1, 1)
        set_const(2 * block + 1, mean, dev)
        for slot in (FAR, NEAR, NEARHALO):
            act_temporal(block, slot, True)
        temporal(block, 1)
        if block == 0:
            start(near_copies(1, skip)[:2])
            start(edge_copies(1, skip, 1))
            start(near_copies(1, skip)[2:])
        far_copy(block, 0).wait_recv()
        far_copy(block, 1).wait_recv()
        act_temporal(block, FARHALO, has_far)
        temporal(block, 0)
        if block == 0:
            start(edge_copies(1, skip, 0))
            tile = local_tile(lambda a, i: skip[a, 1 + i])

    for c in started:
        c.wait_send()
    for block in range(2):
        for j in range(2):
            far_copy(block, j).wait_send()
    for k in range(4):
        for phase in range(2):
            s = slots.at[k, phase]
            pltpu.make_async_copy(s.at[pl.ds(0, 15)], s.at[pl.ds(0, 15)], ar_s.at[k, phase]).wait()


def local(latents, hint, norm_gains, norm_shifts, spatial_kernels, temporal_kernels, zero_weight):
    vmem = pl.BlockSpec(memory_space=pltpu.VMEM)
    hbm = pl.BlockSpec(memory_space=pl.ANY)
    dma = pltpu.SemaphoreType.DMA
    out = pl.pallas_call(
        kernel,
        out_shape=jax.ShapeDtypeStruct((2, 4, C, W), F32),
        in_specs=[vmem] * 4 + [hbm] * 3,
        out_specs=vmem,
        scratch_shapes=[
            pltpu.VMEM((3, 6, C, L), F32),
            pltpu.VMEM((3, 6, C, L), F32),
            pltpu.VMEM((2, 4, 4, C, L), F32),
            pltpu.VMEM((3, K, 6 * L), BF16),
            pltpu.VMEM((4, K, 4 * L), BF16),
            pltpu.VMEM((25, C, C), F32),
            pltpu.VMEM((2, K, 3 * K), BF16),
            pltpu.VMEM((2, C, 3 * K), BF16),
            pltpu.VMEM((C, K), BF16),
            pltpu.VMEM((8, C, L), F32),
            pltpu.VMEM((3, C, L), F32),
            pltpu.VMEM((4, 2, 16, 8, L), F32),
            dma((25,)),
            dma((4, 2)),
            dma((4, 2)),
            dma((12,)),
            dma((12,)),
            dma((6,)),
            dma((6,)),
            dma((4,)),
            dma((4,)),
        ],
        compiler_params=pltpu.CompilerParams(
            collective_id=1, has_side_effects=True, vmem_limit_bytes=60 * 1024 * 1024
        ),
    )(
        jnp.swapaxes(latents, 2, 3), jnp.swapaxes(hint, 2, 3), norm_gains, norm_shifts,
        spatial_kernels, temporal_kernels, zero_weight,
    )
    return jnp.swapaxes(out, 2, 3)


def solution(mesh):
    return jax.shard_map(
        local,
        mesh=mesh,
        in_specs=(
            P("frame", "row", None, None),
            P("frame", "row", None, None),
            P(),
            P(),
            P(),
            P(),
            P(),
        ),
        out_specs=P("frame", "row", None, None),
        check_vma=False,
    )
```

time: 779 us -> 130 us (0.17); the launches traced: 771 us -> 130 us
  blocking collectives: 603 us -> 0 us
  Pallas kernels: 0 us -> 127 us
  matrix products: 65.7 us -> 0 us
  waiting for transfers between devices: 44.4 us -> 0 us
  starting transfers between devices: 24.3 us -> 0 us
  local copies, waits for them, and re-layouts: 23.5 us -> 2.47 us
  other arithmetic: 8.81 us -> 0 us
    psum x8 -> x0, blocking collectives: 603 us -> none  [the longest x4 312 us: group_moments(): totals = lax.psum(jnp.sum(grouped, axis=(0, 2)), ('frame', 'row'))]
    pallas_call x0 -> x1, Pallas kernels: none -> 127 us  [local(): pl.pallas_call(kernel, out_shape=jax.ShapeDtypeStruct((2, 4, C, W), F32),...]
    dot_general x25 -> x0, matrix products: 65.7 us -> none  [the longest x18 47.7 us: spatial_taps(): jnp.einsum('fhwc,cd->fhwd', padded[:, shift_y:shift_y + rows, shift_x:shi...]
    ppermute x8 -> x0, waiting for transfers between devices: 44.4 us -> none  [the longest x4 22.2 us: extended(): after = lax.ppermute(first, axis, down)]
    ppermute x8 -> x0, starting transfers between devices: 24.3 us -> none  [the longest x4 16.8 us: extended(): before = lax.ppermute(last, axis, up)]
    unnamed x20 -> x1, local copies, waits for them, and re-layouts: 12.3 us -> 2.47 us
    slice x6 -> x0, local copies, waits for them, and re-layouts: 8.92 us -> none  [the longest x1 7.77 us: local(): inner = spatial_taps(padded, spatial_kernels[1])]
  transfers between devices with their start and end apart: 8 -> 0, of which waited for: 5 -> 0; matrix products, arithmetic and copies ran while one was open for 4% -> 0% of each run, Pallas kernels for 0% -> 0%
where the time goes in v2:
time: 130 us
  Pallas kernels  127 us (98%)
  local copies, waits for them, and re-layouts  2.47 us (2%)
    pallas_call x1, Pallas kernels, local(): pl.pallas_call(kernel, out_shape=jax.ShapeDtypeStruct((2, 4, C, W), F32),...  127 us

profile of v2, /device:TPU:1, one launch (start us, length us, event | category | flops | bytes accessed | tf_op | source)
XLA Modules:
  0.0 130.0 jit_solution(15315611368464302402)
XLA Ops:
  0.0 127.5 %shard_map.73 = f32[2,4,320,112]{3,2,1,0:T(8,128)} custom-call(f32[2,4,320,112]{3,2,1,0:T(8,128)} %bitcast.4, f32[2,4,320,112]{3,2,1,0:T(8,128)} %bitcast.5, f32[4,320]{1,0:T(4,128)} %gain_ref.1, f32[4,320]{1,0:T(4,128)} %shift_ref.1, f32[2,3,3,320,320]{4,3,2,1,0:T(8,128)} %sk_hbm.1, f32[2,3,320,320]{3,2,1,0:T(8,128)} %tk_hbm.1, f32[320,320]{1,0:T(8,128)} %zw_hbm.1), custom_call_target="tpu_custom_call" | custom-call | tf_op jit(solution)/shard_map/pallas_call | solution.py:324
  127.5 2.5 %copy.9 = f32[2,4,112,320]{2,3,1,0:T(8,128)} copy(f32[2,4,112,320]{2,3,1,0:T(8,128)} %bitcast.3) | data formatting | bytes 2293760

commit v3 on v2

--- a/solution.py
+++ b/solution.py
@@ -26,9 +26,9 @@
 
 
 def kernel(
-    lat_ref, hint_ref, gain_ref, shift_ref, sk_hbm, tk_hbm, zw_hbm, out_ref,
-    ci, skip, inner, act, tact, wst, wsp, wtm, wz, cols, const, slots,
-    wsem, ar_s, ar_r, row_s, row_r, near_s, near_r, far_s, far_r,
+    lat_hbm, hint_hbm, gain_ref, shift_ref, sk_hbm, tk_hbm, zw_hbm, out_ref,
+    lat_ref, hint_ref, ci, skip, inner, act, tact, wst, wsp, wtm, wz, cols, const, slots,
+    in_sem, wsem, ar_s, ar_r, row_s, row_r, near_s, near_r, far_s, far_r,
 ):
     f, r = lax.axis_index("frame"), lax.axis_index("row")
     odd = lax.rem(f, 2)
@@ -42,6 +42,13 @@
     for d in range(1, 16):
         pl.semaphore_signal(barrier, inc=1, device_id=(f, lax.rem(r + d, 16)), device_id_type=MESH)
         pl.semaphore_signal(barrier, inc=1, device_id=(lax.rem(f + d, 16), r), device_id_type=MESH)
+
+    inputs = [
+        pltpu.make_async_copy(lat_hbm, lat_ref, in_sem.at[0]),
+        pltpu.make_async_copy(hint_hbm, hint_ref, in_sem.at[1]),
+    ]
+    for c in inputs:
+        c.start()
 
     weight_copies = []
     for j in range(2):
@@ -75,6 +82,9 @@
         b = lax.broadcasted_iota(jnp.int32, (C, C), 1)
         return jnp.where(a == b, 1.0, 0.0).astype(dtype)
 
+    for c in inputs:
+        c.wait()
+
     for slot, at in ((0, far_at), (1, near_at)):
         for i in range(4):
             ci[slot, 1 + i] = jnp.zeros((C, L), F32)
@@ -142,18 +152,12 @@
             remote(buf.at[slot, 1], buf.at[slot, 5], row_s, row_r, block * 6 + slot * 2 + 1, (f, above)),
         ]
 
-    def near_copies(block, buf):
-        dev = (partner, r)
-        return [
-            remote(buf.at[1, 1], buf.at[2, 1], near_s, near_r, block * 3, dev),
-            remote(buf.at[1, 4], buf.at[2, 4], near_s, near_r, block * 3 + 1, dev),
-            remote(buf.at[1, pl.ds(2, 2)], buf.at[2, pl.ds(2, 2)], near_s, near_r, block * 3 + 2, dev),
-        ]
-
-    def far_copy(block, j):
+    def near_copy(block, buf, i):
+        return remote(buf.at[1, 1 + i], buf.at[2, 1 + i], near_s, near_r, block * 4 + i, (partner, r))
+
+    def far_copy(block, i):
         return remote(
-            inner.at[block, FAR, pl.ds(2 * j, 2)], inner.at[block, FARHALO, pl.ds(2 * j, 2)],
-            far_s, far_r, block * 2 + j, (outer, r),
+            inner.at[block, FAR, i], inner.at[block, FARHALO, i], far_s, far_r, block * 4 + i, (outer, r)
         )
 
     def start(copies):
@@ -205,8 +209,6 @@
                 part = y[:, h * L : (h + 1) * L]
                 o = part[C : 2 * C] + pltpu.roll(part[0:C], 1, 1) + pltpu.roll(part[2 * C : K], L - 1, 1)
                 inner[block, dst, 2 * j + h] = jnp.where(inside, o, 0.0)
-            if dst == FAR:
-                far_copy(block, j).start()
             return 0
 
         lax.fori_loop(0, 2, body, 0)
@@ -250,56 +252,70 @@
                 cols[2 * k + i] = jnp.broadcast_to(col, (C, L))
 
     tile = local_tile(lambda a, i: ci[a, 1 + i])
+    gain_columns()
+    prep_spatial(0, 0)
     pl.semaphore_wait(barrier, 30)
 
     for block, buf in ((0, ci), (1, skip)):
+        edges = [edge_copies(block, buf, slot) for slot in range(3)]
+        near = [near_copy(block, buf, i) for i in range(4)]
+        far = [far_copy(block, i) for i in range(4)]
         ar_send(2 * block, 0, tile)
-        edges = [edge_copies(block, buf, slot) for slot in range(3)]
-        nears = near_copies(block, buf)
-        if block == 0:
-            start(nears[:2])
-            start(edges[1])
-            start(edges[0])
-            start(nears[2:])
-            gain_columns()
-        prep_spatial(block, 0)
+        if block == 0:
+            start(edges[0] + edges[1])
+            start(near[0:1])
+            prep_spatial(block, 1)
+        else:
+            start(near[3:4])
+            prep_spatial(block, 0)
         mean, dev = ar_wait(2 * block, 0)
         ar_send(2 * block, 1, pack(mean, dev))
-        prep_spatial(block, 1)
+        if block == 0:
+            start([near[3], near[1]])
+            prep_small(wz, [24])
+        else:
+            start(near[1:3])
+            prep_spatial(block, 1)
         prep_spatial(block, 2)
-        nears[0].wait_recv()
-        nears[1].wait_recv()
-        start(edges[2])
         mean, dev = ar_wait(2 * block, 1)
         set_const(2 * block, mean, dev)
-        for slot, dst in ((0, FAR), (1, NEAR)):
-            for c in edges[slot]:
-                c.wait_recv()
-            act_frame(buf, slot)
-            spatial(block, slot, dst)
+        if block == 0:
+            start(near[2:3])
+        for c in edges[0]:
+            c.wait_recv()
+        act_frame(buf, 0)
+        spatial(block, 0, FAR)
+        start(far[0:1])
+        near[0].wait_recv()
+        near[3].wait_recv()
+        start(edges[2])
+        for c in edges[1]:
+            c.wait_recv()
+        act_frame(buf, 1)
+        spatial(block, 1, NEAR)
         tile = local_tile(lambda a, i: inner[block, FAR + a, i])
         ar_send(2 * block + 1, 0, tile)
+        start(far[1:2])
+        prep_small(wtm.at[block], [18 + 3 * block + t for t in range(3)])
         for c in edges[2]:
             c.wait_recv()
-        nears[2].wait_recv()
+        near[1].wait_recv()
+        near[2].wait_recv()
         act_frame(buf, 2)
-        spatial(block, 2, NEARHALO)
         mean, dev = ar_wait(2 * block + 1, 0)
         ar_send(2 * block + 1, 1, pack(mean, dev))
-        prep_small(wtm.at[block], [18 + 3 * block + t for t in range(3)])
-        if block == 0:
-            prep_small(wz, [24])
+        start(far[2:4])
+        spatial(block, 2, NEARHALO)
         mean, dev = ar_wait(2 * block + 1, 1)
         set_const(2 * block + 1, mean, dev)
         for slot in (FAR, NEAR, NEARHALO):
             act_temporal(block, slot, True)
         temporal(block, 1)
         if block == 0:
-            start(near_copies(1, skip)[:2])
+            start([near_copy(1, skip, 0)])
             start(edge_copies(1, skip, 1))
-            start(near_copies(1, skip)[2:])
-        far_copy(block, 0).wait_recv()
-        far_copy(block, 1).wait_recv()
+        for c in far:
+            c.wait_recv()
         act_temporal(block, FARHALO, has_far)
         temporal(block, 0)
         if block == 0:
@@ -308,9 +324,6 @@
 
     for c in started:
         c.wait_send()
-    for block in range(2):
-        for j in range(2):
-            far_copy(block, j).wait_send()
     for k in range(4):
         for phase in range(2):
             s = slots.at[k, phase]
@@ -324,9 +337,11 @@
     out = pl.pallas_call(
         kernel,
         out_shape=jax.ShapeDtypeStruct((2, 4, C, W), F32),
-        in_specs=[vmem] * 4 + [hbm] * 3,
+        in_specs=[hbm] * 2 + [vmem] * 2 + [hbm] * 3,
         out_specs=vmem,
         scratch_shapes=[
+            pltpu.VMEM((2, 4, C, W), F32),
+            pltpu.VMEM((2, 4, C, W), F32),
             pltpu.VMEM((3, 6, C, L), F32),
             pltpu.VMEM((3, 6, C, L), F32),
             pltpu.VMEM((2, 4, 4, C, L), F32),
@@ -339,15 +354,16 @@
             pltpu.VMEM((8, C, L), F32),
             pltpu.VMEM((3, C, L), F32),
             pltpu.VMEM((4, 2, 16, 8, L), F32),
+            dma((2,)),
             dma((25,)),
             dma((4, 2)),
             dma((4, 2)),
             dma((12,)),
             dma((12,)),
-            dma((6,)),
-            dma((6,)),
-            dma((4,)),
-            dma((4,)),
+            dma((8,)),
+            dma((8,)),
+            dma((8,)),
+            dma((8,)),
         ],
         compiler_params=pltpu.CompilerParams(
             collective_id=1, has_side_effects=True, vmem_limit_bytes=60 * 1024 * 1024

time: 130 us -> 109 us (0.84)
  Pallas kernels: 127 us -> 106 us
    pallas_call x1, Pallas kernels: 127 us -> 106 us  [local(): pl.pallas_call(kernel, out_shape=jax.ShapeDtypeStruct((2, 4, C, W), F32),...]
where the time goes in v3:
time: 109 us
  Pallas kernels  106 us (97%)
  local copies, waits for them, and re-layouts  2.47 us (2%)
    pallas_call x1, Pallas kernels, local(): pl.pallas_call(kernel, out_shape=jax.ShapeDtypeStruct((2, 4, C, W), F32),...  106 us
    unnamed x1, local copies, waits for them, and re-layouts  2.47 us

profile of v3, /device:TPU:1, one launch (start us, length us, event | category | flops | bytes accessed | tf_op | source)
XLA Modules:
  0.0 108.7 jit_solution(13034096371026400056)
XLA Ops:
  0.0 106.2 %shard_map.73 = f32[2,4,320,112]{3,2,1,0:T(8,128)} custom-call(f32[2,4,320,112]{3,2,1,0:T(8,128)} %bitcast.4, f32[2,4,320,112]{3,2,1,0:T(8,128)} %bitcast.5, f32[4,320]{1,0:T(4,128)} %gain_ref.1, f32[4,320]{1,0:T(4,128)} %shift_ref.1, f32[2,3,3,320,320]{4,3,2,1,0:T(8,128)} %sk_hbm.1, f32[2,3,320,320]{3,2,1,0:T(8,128)} %tk_hbm.1, f32[320,320]{1,0:T(8,128)} %zw_hbm.1), custom_call_target="tpu_custom_call" | custom-call | tf_op jit(solution)/shard_map/pallas_call | solution.py:337
  106.2 2.5 %copy.9 = f32[2,4,112,320]{2,3,1,0:T(8,128)} copy(f32[2,4,112,320]{2,3,1,0:T(8,128)} %bitcast.3) | data formatting | bytes 2293760

commit v4 on v3

--- a/solution.py
+++ b/solution.py
@@ -15,6 +15,8 @@
 L = 128
 PER = 10
 K = 3 * C
+KEPT = 280
+SPARE = C - KEPT
 ROW_LOCAL = 2 * 4 * W * PER
 
 FARHALO, FAR, NEAR, NEARHALO = range(4)
@@ -23,6 +25,22 @@
 def split(v):
     hi = v.astype(BF16)
     return hi, (v - hi.astype(F32)).astype(BF16)
+
+
+def packed(v):
+    lane = lax.broadcasted_iota(jnp.int32, (KEPT, L), 1)
+    last = v[KEPT:C]
+    moved = jnp.concatenate([pltpu.roll(last, W - 16 * k, 1) for k in range(7)], axis=0)
+    return jnp.concatenate([jnp.where(lane < W, v[0:KEPT], moved), last], axis=0)
+
+
+def unpacked(v):
+    lane = lax.broadcasted_iota(jnp.int32, (SPARE, L), 1)
+    last = jnp.zeros((SPARE, L), F32)
+    for k in range(7):
+        moved = pltpu.roll(v[SPARE * k : SPARE * (k + 1)], 16 * k + 16, 1)
+        last = jnp.where((lane >= 16 * k) & (lane < 16 * k + 16), moved, last)
+    return jnp.concatenate([v, last], axis=0)
 
 
 def kernel(
@@ -92,9 +110,10 @@
             v = lat_ref[at, i]
             skip[slot, 1 + i, :, 0:W] = v
             ci[slot, 1 + i, :, 0:W] = v + hint_ref[at, i]
+            ci[slot, 1 + i] = packed(ci[slot, 1 + i])
 
     def local_tile(read):
-        total = lax.fori_loop(0, 8, lambda i, a: a + read(i // 4, lax.rem(i, 4)), jnp.zeros((C, L), F32))
+        total = lax.fori_loop(0, 8, lambda i, a: a + jnp.where(inside, read(i // 4, lax.rem(i, 4)), 0.0), jnp.zeros((C, L), F32))
         mean = to_groups(jnp.sum(total, axis=1, keepdims=True)) * (1.0 / ROW_LOCAL)
         col = to_channels(mean)
 
@@ -146,19 +165,21 @@
 
     started = []
 
+    def sent(buf, slot, i):
+        return buf.at[slot, i, pl.ds(0, KEPT)]
+
     def edge_copies(block, buf, slot):
         return [
-            remote(buf.at[slot, 4], buf.at[slot, 0], row_s, row_r, block * 6 + slot * 2, (f, below)),
-            remote(buf.at[slot, 1], buf.at[slot, 5], row_s, row_r, block * 6 + slot * 2 + 1, (f, above)),
+            remote(sent(buf, slot, 4), sent(buf, slot, 0), row_s, row_r, block * 6 + slot * 2, (f, below)),
+            remote(sent(buf, slot, 1), sent(buf, slot, 5), row_s, row_r, block * 6 + slot * 2 + 1, (f, above)),
         ]
 
     def near_copy(block, buf, i):
-        return remote(buf.at[1, 1 + i], buf.at[2, 1 + i], near_s, near_r, block * 4 + i, (partner, r))
+        return remote(sent(buf, 1, 1 + i), sent(buf, 2, 1 + i), near_s, near_r, block * 4 + i, (partner, r))
 
     def far_copy(block, i):
-        return remote(
-            inner.at[block, FAR, i], inner.at[block, FARHALO, i], far_s, far_r, block * 4 + i, (outer, r)
-        )
+        own = inner.at[block]
+        return remote(sent(own, FAR, i), sent(own, FARHALO, i), far_s, far_r, block * 4 + i, (outer, r))
 
     def start(copies):
         for c in copies:
@@ -190,7 +211,7 @@
     def act_frame(buf, slot):
         def body(i, _):
             ok = ((i > 0) | (r > 0)) & ((i < 5) | (r < 15))
-            hi, lo = activated(buf[slot, i], ok)
+            hi, lo = activated(unpacked(buf[slot, i, 0:KEPT]), ok)
             at = pl.ds(pl.multiple_of(i * L, L), L)
             act[slot, 0:C, at] = hi
             act[slot, C : 2 * C, at] = lo
@@ -208,14 +229,15 @@
             for h in range(2):
                 part = y[:, h * L : (h + 1) * L]
                 o = part[C : 2 * C] + pltpu.roll(part[0:C], 1, 1) + pltpu.roll(part[2 * C : K], L - 1, 1)
-                inner[block, dst, 2 * j + h] = jnp.where(inside, o, 0.0)
+                inner[block, dst, 2 * j + h] = packed(o) if dst == FAR else o
             return 0
 
         lax.fori_loop(0, 2, body, 0)
 
     def act_temporal(block, slot, ok):
         def body(i, _):
-            hi, lo = activated(inner[block, slot, i], ok)
+            v = unpacked(inner[block, slot, i, 0:KEPT]) if slot == FARHALO else inner[block, slot, i]
+            hi, lo = activated(v, ok)
             at = pl.ds(pl.multiple_of(i * L, L), L)
             tact[slot, 0:C, at] = hi
             tact[slot, C : 2 * C, at] = lo
@@ -235,7 +257,7 @@
                 hi, lo = split(co)
                 z = jnp.dot(wz[...], jnp.concatenate([hi, lo, hi], axis=0), preferred_element_type=F32)
                 for h in range(2):
-                    skip[own, rows[h]] = skip[own, rows[h]] + jnp.where(inside, z[:, h * L : (h + 1) * L], 0.0)
+                    skip[own, rows[h]] = packed(skip[own, rows[h]] + z[:, h * L : (h + 1) * L])
             else:
                 for h in range(2):
                     o = skip[own, rows[h]] + y[:, h * L : (h + 1) * L]
@@ -266,6 +288,7 @@
             start(near[0:1])
             prep_spatial(block, 1)
         else:
+            start(edges[0])
             start(near[3:4])
             prep_spatial(block, 0)
         mean, dev = ar_wait(2 * block, 0)
@@ -285,7 +308,7 @@
             c.wait_recv()
         act_frame(buf, 0)
         spatial(block, 0, FAR)
-        start(far[0:1])
+        start(far[0:2])
         near[0].wait_recv()
         near[3].wait_recv()
         start(edges[2])
@@ -295,7 +318,7 @@
         spatial(block, 1, NEAR)
         tile = local_tile(lambda a, i: inner[block, FAR + a, i])
         ar_send(2 * block + 1, 0, tile)
-        start(far[1:2])
+        start(far[2:3])
         prep_small(wtm.at[block], [18 + 3 * block + t for t in range(3)])
         for c in edges[2]:
             c.wait_recv()
@@ -304,7 +327,7 @@
         act_frame(buf, 2)
         mean, dev = ar_wait(2 * block + 1, 0)
         ar_send(2 * block + 1, 1, pack(mean, dev))
-        start(far[2:4])
+        start(far[3:4])
         spatial(block, 2, NEARHALO)
         mean, dev = ar_wait(2 * block + 1, 1)
         set_const(2 * block + 1, mean, dev)
@@ -319,7 +342,6 @@
         act_temporal(block, FARHALO, has_far)
         temporal(block, 0)
         if block == 0:
-            start(edge_copies(1, skip, 0))
             tile = local_tile(lambda a, i: skip[a, 1 + i])
 
     for c in started:

time: 109 us -> 108 us (level)
  no operation moved by 1% of the time
where the time goes in v4:
time: 108 us
  Pallas kernels  105 us (97%)
  local copies, waits for them, and re-layouts  2.47 us (2%)
    pallas_call x1, Pallas kernels, local(): pl.pallas_call(kernel, out_shape=jax.ShapeDtypeStruct((2, 4, C, W), F32),...  105 us
    unnamed x1, local copies, waits for them, and re-layouts  2.47 us

profile of v4, /device:TPU:1, one launch (start us, length us, event | category | flops | bytes accessed | tf_op | source)
XLA Modules:
  0.0 108.0 jit_solution(2122967280539858426)
XLA Ops:
  0.0 105.5 %shard_map.73 = f32[2,4,320,112]{3,2,1,0:T(8,128)} custom-call(f32[2,4,320,112]{3,2,1,0:T(8,128)} %bitcast.4, f32[2,4,320,112]{3,2,1,0:T(8,128)} %bitcast.5, f32[4,320]{1,0:T(4,128)} %gain_ref.1, f32[4,320]{1,0:T(4,128)} %shift_ref.1, f32[2,3,3,320,320]{4,3,2,1,0:T(8,128)} %sk_hbm.1, f32[2,3,320,320]{3,2,1,0:T(8,128)} %tk_hbm.1, f32[320,320]{1,0:T(8,128)} %zw_hbm.1), custom_call_target="tpu_custom_call" | custom-call | tf_op jit(solution)/shard_map/pallas_call | solution.py:359
  105.5 2.5 %copy.9 = f32[2,4,112,320]{2,3,1,0:T(8,128)} copy(f32[2,4,112,320]{2,3,1,0:T(8,128)} %bitcast.3) | data formatting | bytes 2293760

commit v5 on v4

--- a/solution.py
+++ b/solution.py
@@ -230,6 +230,13 @@
                 part = y[:, h * L : (h + 1) * L]
                 o = part[C : 2 * C] + pltpu.roll(part[0:C], 1, 1) + pltpu.roll(part[2 * C : K], L - 1, 1)
                 inner[block, dst, 2 * j + h] = packed(o) if dst == FAR else o
+            if dst == FAR:
+
+                @pl.when(j == 0)
+                def _():
+                    far_copy(block, 0).start()
+                    far_copy(block, 1).start()
+
             return 0
 
         lax.fori_loop(0, 2, body, 0)
@@ -283,32 +290,26 @@
         near = [near_copy(block, buf, i) for i in range(4)]
         far = [far_copy(block, i) for i in range(4)]
         ar_send(2 * block, 0, tile)
-        if block == 0:
-            start(edges[0] + edges[1])
-            start(near[0:1])
-            prep_spatial(block, 1)
-        else:
-            start(edges[0])
-            start(near[3:4])
-            prep_spatial(block, 0)
+        start(near[0:1])
+        prep_spatial(block, 1 - block)
         mean, dev = ar_wait(2 * block, 0)
         ar_send(2 * block, 1, pack(mean, dev))
+        start(edges[0])
+        start(near[3:4])
         if block == 0:
-            start([near[3], near[1]])
             prep_small(wz, [24])
         else:
-            start(near[1:3])
             prep_spatial(block, 1)
         prep_spatial(block, 2)
         mean, dev = ar_wait(2 * block, 1)
+        start(edges[1])
+        start(near[1:2])
         set_const(2 * block, mean, dev)
-        if block == 0:
-            start(near[2:3])
         for c in edges[0]:
             c.wait_recv()
         act_frame(buf, 0)
         spatial(block, 0, FAR)
-        start(far[0:2])
+        started.extend(far[0:2])
         near[0].wait_recv()
         near[3].wait_recv()
         start(edges[2])
@@ -318,25 +319,22 @@
         spatial(block, 1, NEAR)
         tile = local_tile(lambda a, i: inner[block, FAR + a, i])
         ar_send(2 * block + 1, 0, tile)
-        start(far[2:3])
+        start(near[2:3])
         prep_small(wtm.at[block], [18 + 3 * block + t for t in range(3)])
+        mean, dev = ar_wait(2 * block + 1, 0)
+        ar_send(2 * block + 1, 1, pack(mean, dev))
+        start(far[2:4])
         for c in edges[2]:
             c.wait_recv()
         near[1].wait_recv()
         near[2].wait_recv()
         act_frame(buf, 2)
-        mean, dev = ar_wait(2 * block + 1, 0)
-        ar_send(2 * block + 1, 1, pack(mean, dev))
-        start(far[3:4])
         spatial(block, 2, NEARHALO)
         mean, dev = ar_wait(2 * block + 1, 1)
         set_const(2 * block + 1, mean, dev)
         for slot in (FAR, NEAR, NEARHALO):
             act_temporal(block, slot, True)
         temporal(block, 1)
-        if block == 0:
-            start([near_copy(1, skip, 0)])
-            start(edge_copies(1, skip, 1))
         for c in far:
             c.wait_recv()
         act_temporal(block, FARHALO, has_far)

time: 108 us -> 116 us (1.074)
  the two profiles are of different devices: /device:TPU:1 before, /device:TPU:56 now
where the time goes in v5:
time: 116 us
  Pallas kernels  113 us (97%)
  local copies, waits for them, and re-layouts  2.47 us (2%)
    pallas_call x1, Pallas kernels, local(): pl.pallas_call(kernel, out_shape=jax.ShapeDtypeStruct((2, 4, C, W), F32),...  113 us
    unnamed x1, local copies, waits for them, and re-layouts  2.47 us

profile of v5, /device:TPU:56, one launch (start us, length us, event | category | flops | bytes accessed | tf_op | source)
XLA Modules:
  0.0 115.9 jit_solution(6526718989507588835)
XLA Ops:
  0.0 113.4 %shard_map.73 = f32[2,4,320,112]{3,2,1,0:T(8,128)} custom-call(f32[2,4,320,112]{3,2,1,0:T(8,128)} %bitcast.4, f32[2,4,320,112]{3,2,1,0:T(8,128)} %bitcast.5, f32[4,320]{1,0:T(4,128)} %gain_ref.1, f32[4,320]{1,0:T(4,128)} %shift_ref.1, f32[2,3,3,320,320]{4,3,2,1,0:T(8,128)} %sk_hbm.1, f32[2,3,320,320]{3,2,1,0:T(8,128)} %tk_hbm.1, f32[320,320]{1,0:T(8,128)} %zw_hbm.1), custom_call_target="tpu_custom_call" | custom-call | tf_op jit(solution)/shard_map/pallas_call | solution.py:357
  113.4 2.5 %copy.9 = f32[2,4,112,320]{2,3,1,0:T(8,128)} copy(f32[2,4,112,320]{2,3,1,0:T(8,128)} %bitcast.3) | data formatting | bytes 2293760

commit v6 on v4

--- a/solution.py
+++ b/solution.py
@@ -156,7 +156,7 @@
 
     def activated(v, ok):
         u = (v - const[0]) * const[1] + const[2]
-        return split(jnp.where(inside & ok, u / (1.0 + jnp.exp(-u)), 0.0))
+        return split(jnp.where(inside & ok, 0.5 * u + 0.5 * u * jnp.tanh(0.5 * u), 0.0))
 
     def remote(src, dst, sends, recvs, at, device):
         return pltpu.make_async_remote_copy(
@@ -230,6 +230,13 @@
                 part = y[:, h * L : (h + 1) * L]
                 o = part[C : 2 * C] + pltpu.roll(part[0:C], 1, 1) + pltpu.roll(part[2 * C : K], L - 1, 1)
                 inner[block, dst, 2 * j + h] = packed(o) if dst == FAR else o
+            if dst == FAR:
+
+                @pl.when(j == 0)
+                def _():
+                    far_copy(block, 0).start()
+                    far_copy(block, 1).start()
+
             return 0
 
         lax.fori_loop(0, 2, body, 0)
@@ -285,7 +292,7 @@
         ar_send(2 * block, 0, tile)
         if block == 0:
             start(edges[0] + edges[1])
-            start(near[0:1])
+            start([near[0], near[3]])
             prep_spatial(block, 1)
         else:
             start(edges[0])
@@ -294,7 +301,7 @@
         mean, dev = ar_wait(2 * block, 0)
         ar_send(2 * block, 1, pack(mean, dev))
         if block == 0:
-            start([near[3], near[1]])
+            start(near[1:3])
             prep_small(wz, [24])
         else:
             start(near[1:3])
@@ -302,13 +309,11 @@
         prep_spatial(block, 2)
         mean, dev = ar_wait(2 * block, 1)
         set_const(2 * block, mean, dev)
-        if block == 0:
-            start(near[2:3])
         for c in edges[0]:
             c.wait_recv()
         act_frame(buf, 0)
         spatial(block, 0, FAR)
-        start(far[0:2])
+        started.extend(far[0:2])
         near[0].wait_recv()
         near[3].wait_recv()
         start(edges[2])
@@ -318,7 +323,6 @@
         spatial(block, 1, NEAR)
         tile = local_tile(lambda a, i: inner[block, FAR + a, i])
         ar_send(2 * block + 1, 0, tile)
-        start(far[2:3])
         prep_small(wtm.at[block], [18 + 3 * block + t for t in range(3)])
         for c in edges[2]:
             c.wait_recv()
@@ -327,7 +331,7 @@
         act_frame(buf, 2)
         mean, dev = ar_wait(2 * block + 1, 0)
         ar_send(2 * block + 1, 1, pack(mean, dev))
-        start(far[3:4])
+        start(far[2:4])
         spatial(block, 2, NEARHALO)
         mean, dev = ar_wait(2 * block + 1, 1)
         set_const(2 * block + 1, mean, dev)

time: 108 us -> 108 us (level)
  no operation moved by 1% of the time
where the time goes in v6:
time: 108 us
  Pallas kernels  105 us (97%)
  local copies, waits for them, and re-layouts  2.47 us (2%)
    pallas_call x1, Pallas kernels, local(): pl.pallas_call(kernel, out_shape=jax.ShapeDtypeStruct((2, 4, C, W), F32),...  105 us
    unnamed x1, local copies, waits for them, and re-layouts  2.47 us

profile of v6, /device:TPU:1, one launch (start us, length us, event | category | flops | bytes accessed | tf_op | source)
XLA Modules:
  0.0 107.7 jit_solution(15352511638943214562)
XLA Ops:
  0.0 105.2 %shard_map.73 = f32[2,4,320,112]{3,2,1,0:T(8,128)} custom-call(f32[2,4,320,112]{3,2,1,0:T(8,128)} %bitcast.4, f32[2,4,320,112]{3,2,1,0:T(8,128)} %bitcast.5, f32[4,320]{1,0:T(4,128)} %gain_ref.1, f32[4,320]{1,0:T(4,128)} %shift_ref.1, f32[2,3,3,320,320]{4,3,2,1,0:T(8,128)} %sk_hbm.1, f32[2,3,320,320]{3,2,1,0:T(8,128)} %tk_hbm.1, f32[320,320]{1,0:T(8,128)} %zw_hbm.1), custom_call_target="tpu_custom_call" | custom-call | tf_op jit(solution)/shard_map/pallas_call | solution.py:363
  105.2 2.5 %copy.9 = f32[2,4,112,320]{2,3,1,0:T(8,128)} copy(f32[2,4,112,320]{2,3,1,0:T(8,128)} %bitcast.3) | data formatting | bytes 2293760
